TPU v7x, 32 devices: a whole 2x2x4 slice. The times are simulated.
32 devices in a mesh: groups: 2 (over y), rows: 16 (over z, x, core).
Axes of the slice: x: 2, y: 2, z: 4, core: 2. Of those that a mesh axis runs over, the one named last changes fastest.
Arguments:
- transition_tiles: bfloat16 [2048, 5, 128, 128], P(('groups', 'rows')), parts along dimension 0, may hold values from 0.049804688 to 1
- column_tiles: int32 [2048, 5], P(('groups', 'rows')), parts along dimension 0, may hold values from 0 to 1023, as said below
- schur_basis: bfloat16 [32, 262144], P(None, ('groups', 'rows')), parts along dimension 1, may hold values from -60 to 60
- membership_map: float32 [64, 32], P('groups'), parts along dimension 0, may hold values from -1 to 1
Outputs:
- memberships: float32 [32, 262144], P(None, ('groups', 'rows')), parts along dimension 1
There are 2 independent parts, one for each index of `groups`. A program takes and returns all parts, laid end to end along the dimension named above; each array names one. Nothing has to cross between parts.
Inputs may be any that keep to these rules, and one draw needn't show every extreme that they name: `column_tiles`: the 5 entries of row tile r are distinct column tiles, r itself among them, all within 64 of r; some row tile has one at distance exactly 64.
All inputs are finite; a program needn't handle non-finite values.
Results may differ from a plain program's by a relative error of at most 0.0045.
Values may be sent and summed in bfloat16 or wider, within the bound.
No kernel may reach another device: no remote copies, remote signals or barrier semaphores. Data moves between devices by JAX's collectives and lax.ppermute only.
A program may use at most 64 MiB of HBM per device.

v0:
```python
import jax
import jax.numpy as jnp
from jax import lax
from jax.sharding import PartitionSpec as P

PRODUCTS = 4


def padded_2(block, sides, width):
    for axis, dim in sides:
        count = lax.axis_size(axis)
        forward = [(i, i + 1) for i in range(count - 1)]
        backward = [(target, source) for source, target in forward]
        low = lax.ppermute(
            lax.slice_in_dim(block, block.shape[dim] - width, None, axis=dim), axis, forward
        )
        high = lax.ppermute(lax.slice_in_dim(block, 0, width, axis=dim), axis, backward)
        block = jnp.concatenate([low, block, high], axis=dim)
    return block


def tile_product(transition_tiles, local_index, row_total, padded):
    vector_count = padded.shape[0]
    tile_size = transition_tiles.shape[-1]
    blocks = padded.reshape(vector_count, -1, tile_size)
    picked = jnp.take(blocks, local_index, axis=1)
    summed = jnp.einsum(
        "rsij,vrsj->vri", transition_tiles, picked, preferred_element_type=jnp.float32
    )
    return (summed / row_total[None]).reshape(vector_count, -1)


def body(transition_tiles, column_tiles, schur_basis, membership_map):
    panel_tiles = transition_tiles.shape[0]
    tile_size = transition_tiles.shape[-1]
    shard_width = schur_basis.shape[1]
    state_count = shard_width * lax.axis_size("rows")
    own_first = lax.axis_index("rows") * panel_tiles
    first_tile = own_first - panel_tiles
    local_index = column_tiles - first_tile
    unit_vector = jnp.ones((tile_size,), jnp.bfloat16)
    row_total = jnp.einsum(
        "rsij,j->ri", transition_tiles, unit_vector, preferred_element_type=jnp.float32
    )
    padded = padded_2(schur_basis, (("rows", 1),), shard_width)
    result = tile_product(transition_tiles, local_index, row_total, padded)
    for step in range(PRODUCTS - 1):
        image = result.astype(jnp.bfloat16)
        padded_image = padded_2(image, (("rows", 1),), shard_width)
        result = tile_product(transition_tiles, local_index, row_total, padded_image)
    gram_local = (
        jnp.dot(
            result, result.T, precision=lax.Precision.HIGHEST, preferred_element_type=jnp.float32
        )
        / state_count
    )
    gram_total = lax.psum(gram_local, "rows")
    factor = jnp.linalg.cholesky(gram_total)
    basis_q = jax.scipy.linalg.solve_triangular(factor, result, lower=True)
    return jnp.dot(
        membership_map.T,
        basis_q,
        precision=lax.Precision.HIGHEST,
        preferred_element_type=jnp.float32,
    )


def solution(mesh):
    return jax.shard_map(
        body,
        mesh=mesh,
        in_specs=(
            P(("groups", "rows"), None, None, None),
            P(("groups", "rows"), None),
            P(None, ("groups", "rows")),
            P("groups", None),
        ),
        out_specs=P(None, ("groups", "rows")),
        check_vma=False,
    )
```

profile of v0, /device:TPU:0, one launch (start us, length us, event | category | flops | bytes accessed | tf_op | source)
XLA Modules:
  0.0 183.3 jit_solution(8848551696498775349)
XLA Ops:
  0.0 2.5 %collective-permute-start = (bf16[32,8192]{1,0:T(8,128)(2,1)}, bf16[32,8192]{1,0:T(8,128)(2,1)S(1)}, u32[]{:S(2)}, u32[]{:S(2)}) collective-permute-start(bf16[32,8192]{1,0:T(8,128)(2,1)} %param.8), channel_id=1, source_target_pairs={{0,1},{1,2},{2,3},{3,4},{4,5},{5,6},{6,7},{7,8},{8,9},{9,10},{10,1... | collective-permute-start | bytes 1572872 | tf_op jit(solution)/shard_map/ppermute | solution.py:14
  2.5 1.3 collective-permute-start.1
  3.8 6.6 %convert_reduce_fusion = bf16[64,128,128]{2,1,0:T(8,128)(2,1)S(1)} fusion(bf16[64,5,128,128]{3,2,1,0:T(8,128)(2,1)} %param.6), kind=kLoop, calls=%fused_computation.4 | loop fusion | flops 9437184 | bytes 12582912 | tf_op jit(solution)/shard_map/rsij,j->ri/reduce_sum | solution.py:42
  10.8 0.6 fusion.58
  11.5 1.3 copy_bitcast_fusion.3
  12.8 3.0 %gather_fusion = bf16[320,32,128]{2,1,0:T(8,128)(2,1)} fusion(bf16[32,192,128]{2,0,1:T(8,128)(2,1)S(1)} %copy_bitcast_fusion.3, s32[1024]{0:T(1024)S(1)} %pad_clamp_fusion), kind=kCustom, calls=%fused_computation.clone | custom fusion | bytes 5244160 | tf_op jit(solution)/shard_map/jit(_take)/gather | solution.py:26
  15.8 8.5 %fusion.52 = bf16[64,4,8,128]{3,2,1,0:T(8,128)(2,1)S(1)} fusion(bf16[64,5,128,128]{3,2,1,0:T(8,128)(2,1)} %param.6, bf16[64,5,32,128]{3,2,1,0:T(8,128)(2,1)} %bitcast.137, pred[64,5]{1,0:T(8,128)(4,1)S(1)} %copy.26, f32[64,128]{1,0:T(8,128)S(1)} %bitcast.149), kind=kOutput, calls=%fused_computation.50 | convolution fusion | flops 337379328 | bytes 13664576 | tf_op jit(solution)/shard_map/rsij,vrsj->vri/dot_general | solution.py:27
  24.4 1.3 collective-permute-start.3
  25.7 8.2 %collective-permute-start.2 = (bf16[32,8192]{1,0:T(8,128)(2,1)S(1)}, bf16[32,8192]{1,0:T(8,128)(2,1)S(1)}, u32[]{:S(2)}, u32[]{:S(2)}) collective-permute-start(bf16[32,8192]{1,0:T(8,128)(2,1)S(1)} %bitcast.141), channel_id=1, source_target_pairs={{0,1},{1,2},{2,3},{3,4},{4,5},{5,6},{6,7},{7,8},{8,9},{9,10},{10,1... | collective-permute-start | bytes 1572872 | tf_op jit(solution)/shard_map/ppermute | solution.py:14
  34.0 1.5 collective-permute-done.2
  35.4 0.3 copy_bitcast_fusion.2
  35.7 3.0 %gather_fusion.1 = bf16[320,32,128]{2,1,0:T(8,128)(2,1)} fusion(bf16[32,192,128]{2,0,1:T(8,128)(2,1)S(1)} %copy_bitcast_fusion.2, s32[1024]{0:T(1024)S(1)} %pad_clamp_fusion), kind=kCustom, calls=%fused_computation.1.clone | custom fusion | bytes 5244160 | tf_op jit(solution)/shard_map/jit(_take)/gather | solution.py:26
  38.7 8.5 %fusion.47 = bf16[64,4,8,128]{3,2,1,0:T(8,128)(2,1)S(1)} fusion(bf16[64,5,128,128]{3,2,1,0:T(8,128)(2,1)} %param.6, bf16[64,5,32,128]{3,2,1,0:T(8,128)(2,1)} %bitcast.138, pred[64,5]{1,0:T(8,128)(4,1)S(1)} %copy.26, f32[64,128]{1,0:T(8,128)S(1)} %bitcast.150), kind=kOutput, calls=%fused_computation.49 | convolution fusion | flops 337379328 | bytes 13664576 | tf_op jit(solution)/shard_map/rsij,vrsj->vri/dot_general | solution.py:27
  47.3 1.3 collective-permute-start.5
  48.6 13.6 %collective-permute-start.4 = (bf16[32,8192]{1,0:T(8,128)(2,1)S(1)}, bf16[32,8192]{1,0:T(8,128)(2,1)S(1)}, u32[]{:S(2)}, u32[]{:S(2)}) collective-permute-start(bf16[32,8192]{1,0:T(8,128)(2,1)S(1)} %bitcast.144), channel_id=1, source_target_pairs={{0,1},{1,2},{2,3},{3,4},{4,5},{5,6},{6,7},{7,8},{8,9},{9,10},{10,1... | collective-permute-start | bytes 1572872 | tf_op jit(solution)/shard_map/ppermute | solution.py:14
  62.2 1.3 collective-permute-done.4
  63.5 0.3 copy_bitcast_fusion.1
  63.8 3.0 %gather_fusion.2 = bf16[320,32,128]{2,1,0:T(8,128)(2,1)} fusion(bf16[32,192,128]{2,0,1:T(8,128)(2,1)S(1)} %copy_bitcast_fusion.1, s32[1024]{0:T(1024)S(1)} %pad_clamp_fusion), kind=kCustom, calls=%fused_computation.2.clone | custom fusion | bytes 5244160 | tf_op jit(solution)/shard_map/jit(_take)/gather | solution.py:26
  66.8 8.5 %fusion.42 = bf16[64,4,8,128]{3,2,1,0:T(8,128)(2,1)S(1)} fusion(bf16[64,5,128,128]{3,2,1,0:T(8,128)(2,1)} %param.6, bf16[64,5,32,128]{3,2,1,0:T(8,128)(2,1)} %bitcast.139, pred[64,5]{1,0:T(8,128)(4,1)S(1)} %copy.26, f32[64,128]{1,0:T(8,128)S(1)} %bitcast.151), kind=kOutput, calls=%fused_computation.48 | convolution fusion | flops 337379328 | bytes 13664576 | tf_op jit(solution)/shard_map/rsij,vrsj->vri/dot_general | solution.py:27
  75.4 1.3 collective-permute-start.7
  76.7 10.6 %collective-permute-start.6 = (bf16[32,8192]{1,0:T(8,128)(2,1)S(1)}, bf16[32,8192]{1,0:T(8,128)(2,1)S(1)}, u32[]{:S(2)}, u32[]{:S(2)}) collective-permute-start(bf16[32,8192]{1,0:T(8,128)(2,1)S(1)} %bitcast.147), channel_id=1, source_target_pairs={{0,1},{1,2},{2,3},{3,4},{4,5},{5,6},{6,7},{7,8},{8,9},{9,10},{10,1... | collective-permute-start | bytes 1572872 | tf_op jit(solution)/shard_map/ppermute | solution.py:14
  87.3 1.5 collective-permute-done.6
  89.1 3.0 %gather_fusion.3 = bf16[320,32,128]{2,1,0:T(8,128)(2,1)} fusion(bf16[32,192,128]{2,0,1:T(8,128)(2,1)S(1)} %copy_bitcast_fusion, s32[1024]{0:T(1024)S(1)} %pad_clamp_fusion), kind=kCustom, calls=%fused_computation.3.clone | custom fusion | bytes 5244160 | tf_op jit(solution)/shard_map/jit(_take)/gather | solution.py:26
  92.1 8.4 %fusion.37 = f32[64,32,128]{2,1,0:T(8,128)S(1)} fusion(bf16[64,5,128,128]{3,2,1,0:T(8,128)(2,1)} %param.6, bf16[64,5,32,128]{3,2,1,0:T(8,128)(2,1)} %bitcast.136, pred[64,5]{1,0:T(8,128)(4,1)S(1)} %copy.26, f32[64,128]{1,0:T(8,128)S(1)} %bitcast.152), kind=kOutput, calls=%fused_computation.47 | convolution fusion | flops 337117184 | bytes 14188864 | tf_op jit(solution)/shard_map/rsij,vrsj->vri/dot_general | solution.py:27
  100.6 1.0 fusion.32
  101.5 71.9 %psum.7 = f32[32,32]{0,1:T(8,128)S(1)} all-reduce(f32[32,32]{0,1:T(8,128)S(1)} %fusion.32), channel_id=1, replica_groups=mesh['groups'=2,'rows'=16] {'rows'}, use_global_device_ids=true, to_apply=%region_1.0 | all-reduce | flops 1024 | bytes 8192 | tf_op jit(solution)/shard_map/psum | solution.py:57
  173.6 2.9 %cholesky.16 = f32[32,32]{1,0:T(8,128)S(1)} custom-call(f32[32,32]{1,0:T(8,128)S(1)} %fusion.57), custom_call_target="Cholesky" | custom-call | tf_op jit(solution)/shard_map/jit(cholesky)/cholesky | solution.py:58
  176.5 0.6 compare_reduce_fusion
  177.1 0.7 fusion.55
  177.8 2.4 %custom-call.7 = f32[1,32,32]{1,2,0:T(8,128)S(1)} custom-call(f32[1,32,32]{2,1,0:T(8,128)S(1)} %fusion.55), custom_call_target="InvertDiagBlocksLowerTriangular" | custom-call | tf_op jit(solution)/shard_map/jit(_solve_triangular)/triangular_solve | solution.py:59
  180.2 1.1 fusion.33
  181.3 2.0 %convolution_bitcast_fusion = f32[32,8192]{1,0:T(8,128)} fusion(f32[32,8192]{1,0:T(8,128)S(1)} %fusion.33, f32[32,32]{1,0:T(8,128)S(1)} %copy-done), kind=kOutput, calls=%fused_computation.5 | convolution fusion | flops 100663296 | bytes 2101248 | tf_op jit(solution)/shard_map/dot_general | solution.py:60
  (23 shorter events, 1.1 us)
Async XLA Ops:
  0.0 181.3 %copy-start = (f32[32,32]{1,0:T(8,128)S(1)}, f32[32,32]{1,0:T(8,128)}, u32[]{:S(2)}) copy-start(f32[32,32]{1,0:T(8,128)} %param.9) | copy-start | bytes 12292
  0.0 11.5 %collective-permute-start = (bf16[32,8192]{1,0:T(8,128)(2,1)}, bf16[32,8192]{1,0:T(8,128)(2,1)S(1)}, u32[]{:S(2)}, u32[]{:S(2)}) collective-permute-start(bf16[32,8192]{1,0:T(8,128)(2,1)} %param.8), channel_id=1, source_target_pairs={{0,1},{1,2},{2,3},{3,4},{4,5},{5,6},{6,7},{7,8},{8,9},{9,10},{10,1... | collective-permute-start | bytes 1572872 | tf_op jit(solution)/shard_map/ppermute | solution.py:14
  2.5 8.9 %collective-permute-start.1 = (bf16[32,8192]{1,0:T(8,128)(2,1)}, bf16[32,8192]{1,0:T(8,128)(2,1)}, u32[]{:S(2)}, u32[]{:S(2)}) collective-permute-start(bf16[32,8192]{1,0:T(8,128)(2,1)} %param.8), channel_id=1, source_target_pairs={{1,0},{2,1},{3,2},{4,3},{5,4},{6,5},{7,6},{8,7},{9,8},{10,9},{11,1... | collective-permute-start | bytes 1572872 | tf_op jit(solution)/shard_map/ppermute | solution.py:17
  3.8 6.6 %copy-start.2 = (s32[64,5]{0,1:T(8,128)S(1)}, s32[64,5]{0,1:T(8,128)}, u32[]{:S(2)}) copy-start(s32[64,5]{0,1:T(8,128)} %param.7) | copy-start | bytes 3844
  3.8 7.6 %copy-start.1 = (bf16[32,8192]{1,0:T(8,128)(2,1)S(1)}, bf16[32,8192]{1,0:T(8,128)(2,1)}, u32[]{:S(2)}) copy-start(bf16[32,8192]{1,0:T(8,128)(2,1)} %param.8) | copy-start | bytes 1572868
  24.4 9.5 %collective-permute-start.3 = (bf16[32,8192]{1,0:T(8,128)(2,1)S(1)}, bf16[32,8192]{1,0:T(8,128)(2,1)S(1)}, u32[]{:S(2)}, u32[]{:S(2)}) collective-permute-start(bf16[32,8192]{1,0:T(8,128)(2,1)S(1)} %bitcast.140), channel_id=1, source_target_pairs={{1,0},{2,1},{3,2},{4,3},{5,4},{6,5},{7,6},{8,7},{9,8},{10,9},{11,1... | collective-permute-start | bytes 1572872 | tf_op jit(solution)/shard_map/ppermute | solution.py:17
  25.7 9.7 %collective-permute-start.2 = (bf16[32,8192]{1,0:T(8,128)(2,1)S(1)}, bf16[32,8192]{1,0:T(8,128)(2,1)S(1)}, u32[]{:S(2)}, u32[]{:S(2)}) collective-permute-start(bf16[32,8192]{1,0:T(8,128)(2,1)S(1)} %bitcast.141), channel_id=1, source_target_pairs={{0,1},{1,2},{2,3},{3,4},{4,5},{5,6},{6,7},{7,8},{8,9},{9,10},{10,1... | collective-permute-start | bytes 1572872 | tf_op jit(solution)/shard_map/ppermute | solution.py:14
  47.3 14.9 %collective-permute-start.5 = (bf16[32,8192]{1,0:T(8,128)(2,1)S(1)}, bf16[32,8192]{1,0:T(8,128)(2,1)S(1)}, u32[]{:S(2)}, u32[]{:S(2)}) collective-permute-start(bf16[32,8192]{1,0:T(8,128)(2,1)S(1)} %bitcast.143), channel_id=1, source_target_pairs={{1,0},{2,1},{3,2},{4,3},{5,4},{6,5},{7,6},{8,7},{9,8},{10,9},{11,1... | collective-permute-start | bytes 1572872 | tf_op jit(solution)/shard_map/ppermute | solution.py:17
  48.6 14.9 %collective-permute-start.4 = (bf16[32,8192]{1,0:T(8,128)(2,1)S(1)}, bf16[32,8192]{1,0:T(8,128)(2,1)S(1)}, u32[]{:S(2)}, u32[]{:S(2)}) collective-permute-start(bf16[32,8192]{1,0:T(8,128)(2,1)S(1)} %bitcast.144), channel_id=1, source_target_pairs={{0,1},{1,2},{2,3},{3,4},{4,5},{5,6},{6,7},{7,8},{8,9},{9,10},{10,1... | collective-permute-start | bytes 1572872 | tf_op jit(solution)/shard_map/ppermute | solution.py:14
  75.4 11.9 %collective-permute-start.7 = (bf16[32,8192]{1,0:T(8,128)(2,1)S(1)}, bf16[32,8192]{1,0:T(8,128)(2,1)S(1)}, u32[]{:S(2)}, u32[]{:S(2)}) collective-permute-start(bf16[32,8192]{1,0:T(8,128)(2,1)S(1)} %bitcast.146), channel_id=1, source_target_pairs={{1,0},{2,1},{3,2},{4,3},{5,4},{6,5},{7,6},{8,7},{9,8},{10,9},{11,1... | collective-permute-start | bytes 1572872 | tf_op jit(solution)/shard_map/ppermute | solution.py:17
  76.7 12.1 %collective-permute-start.6 = (bf16[32,8192]{1,0:T(8,128)(2,1)S(1)}, bf16[32,8192]{1,0:T(8,128)(2,1)S(1)}, u32[]{:S(2)}, u32[]{:S(2)}) collective-permute-start(bf16[32,8192]{1,0:T(8,128)(2,1)S(1)} %bitcast.147), channel_id=1, source_target_pairs={{0,1},{1,2},{2,3},{3,4},{4,5},{5,6},{6,7},{7,8},{8,9},{9,10},{10,1... | collective-permute-start | bytes 1572872 | tf_op jit(solution)/shard_map/ppermute | solution.py:14
where the time goes:
time: 184 us; the launch traced here: 183 us
  blocking collectives  71.9 us (39%)
  starting transfers between devices  40.1 us (22%)
  matrix products  38.6 us (21%)
  other arithmetic  15.4 us (8%)
  local copies, waits for them, and re-layouts  12.8 us (7%)
  waiting for transfers between devices  4.26 us (2%)
    psum x1, blocking collectives, body(): gram_total = lax.psum(gram_local, 'rows')  71.9 us
    ppermute x4, starting transfers between devices, padded_2(): lax.ppermute(lax.slice_in_dim(block, block.shape[dim] - width, None, axis...  34.9 us
    dot_general x4, matrix products, tile_product(): jnp.einsum('rsij,vrsj->vri', transition_tiles, picked, preferred_element_...  33.9 us
    gather x4, local copies, waits for them, and re-layouts, tile_product(): picked = jnp.take(blocks, local_index, axis=1)  12.1 us
    reduce_sum x1, other arithmetic, body(): jnp.einsum('rsij,j->ri', transition_tiles, unit_vector, preferred_element...  6.58 us
    ppermute x4, starting transfers between devices, padded_2(): lax.ppermute(lax.slice_in_dim(block, 0, width, axis=dim), axis, backward)  5.17 us
    ppermute x4, waiting for transfers between devices, padded_2(): lax.ppermute(lax.slice_in_dim(block, block.shape[dim] - width, None, axis...  4.25 us
  transfers between devices with their start and end apart: 8, of which 3 were waited for; matrix products, arithmetic and copies ran while one was open for 4% of the time, Pallas kernels for 0%

commit v1 on v0

--- a/solution.py
+++ b/solution.py
@@ -54,7 +54,7 @@
         )
         / state_count
     )
-    gram_total = lax.psum(gram_local, "rows")
+    gram_total = jnp.sum(lax.all_gather(gram_local, "rows"), axis=0)
     factor = jnp.linalg.cholesky(gram_total)
     basis_q = jax.scipy.linalg.solve_triangular(factor, result, lower=True)
     return jnp.dot(

time: 184 us -> 147 us (0.80)
  blocking collectives: 71.9 us -> 35.3 us
    psum x1 -> x0, blocking collectives: 71.9 us -> none  [body(): gram_total = lax.psum(gram_local, 'rows')]
    all_gather x0 -> x1, blocking collectives: none -> 35.3 us  [body(): gram_total = jnp.sum(lax.all_gather(gram_local, 'rows'), axis=0)]
  transfers between devices with their start and end apart: 8 -> 8, of which waited for: 3 -> 3; matrix products, arithmetic and copies ran while one was open for 4% -> 5% of each run, Pallas kernels for 0% -> 0%
where the time goes in v1:
time: 147 us
  starting transfers between devices  40.1 us (27%)
  matrix products  38.6 us (26%)
  blocking collectives  35.3 us (24%)
  other arithmetic  15.4 us (10%)
  local copies, waits for them, and re-layouts  12.8 us (9%)
  waiting for transfers between devices  4.26 us (3%)
    all_gather x1, blocking collectives, body(): gram_total = jnp.sum(lax.all_gather(gram_local, 'rows'), axis=0)  35.3 us
    ppermute x4, starting transfers between devices, padded_2(): lax.ppermute(lax.slice_in_dim(block, block.shape[dim] - width, None, axis...  34.9 us
    dot_general x4, matrix products, tile_product(): jnp.einsum('rsij,vrsj->vri', transition_tiles, picked, preferred_element_...  33.9 us
    gather x4, local copies, waits for them, and re-layouts, tile_product(): picked = jnp.take(blocks, local_index, axis=1)  12.1 us
    reduce_sum x1, other arithmetic, body(): jnp.einsum('rsij,j->ri', transition_tiles, unit_vector, preferred_element...  6.58 us
    ppermute x4, starting transfers between devices, padded_2(): lax.ppermute(lax.slice_in_dim(block, 0, width, axis=dim), axis, backward)  5.17 us
    ppermute x4, waiting for transfers between devices, padded_2(): lax.ppermute(lax.slice_in_dim(block, block.shape[dim] - width, None, axis...  4.25 us
    another operation x3, other arithmetic, body(): factor = jnp.linalg.cholesky(gram_total)  3.59 us
  transfers between devices with their start and end apart: 8, of which 3 were waited for; matrix products, arithmetic and copies ran while one was open for 5% of the time, Pallas kernels for 0%

profile of v1, /device:TPU:0, one launch (start us, length us, event | category | flops | bytes accessed | tf_op | source)
XLA Modules:
  0.0 146.7 jit_solution(14275544095782436803)
XLA Ops:
  0.0 2.5 %collective-permute-start = (bf16[32,8192]{1,0:T(8,128)(2,1)}, bf16[32,8192]{1,0:T(8,128)(2,1)S(1)}, u32[]{:S(2)}, u32[]{:S(2)}) collective-permute-start(bf16[32,8192]{1,0:T(8,128)(2,1)} %param.8), channel_id=1, source_target_pairs={{0,1},{1,2},{2,3},{3,4},{4,5},{5,6},{6,7},{7,8},{8,9},{9,10},{10,1... | collective-permute-start | bytes 1572872 | tf_op jit(solution)/shard_map/ppermute | solution.py:14
  2.5 1.3 collective-permute-start.1
  3.8 6.6 %convert_reduce_fusion = bf16[64,128,128]{2,1,0:T(8,128)(2,1)S(1)} fusion(bf16[64,5,128,128]{3,2,1,0:T(8,128)(2,1)} %param.6), kind=kLoop, calls=%fused_computation.4 | loop fusion | flops 9437184 | bytes 12582912 | tf_op jit(solution)/shard_map/rsij,j->ri/reduce_sum | solution.py:42
  10.8 0.6 fusion.58
  11.5 1.3 copy_bitcast_fusion.3
  12.8 3.0 %gather_fusion = bf16[320,32,128]{2,1,0:T(8,128)(2,1)} fusion(bf16[32,192,128]{2,0,1:T(8,128)(2,1)S(1)} %copy_bitcast_fusion.3, s32[1024]{0:T(1024)S(1)} %pad_clamp_fusion), kind=kCustom, calls=%fused_computation.clone | custom fusion | bytes 5244160 | tf_op jit(solution)/shard_map/jit(_take)/gather | solution.py:26
  15.8 8.5 %fusion.52 = bf16[64,4,8,128]{3,2,1,0:T(8,128)(2,1)S(1)} fusion(bf16[64,5,128,128]{3,2,1,0:T(8,128)(2,1)} %param.6, bf16[64,5,32,128]{3,2,1,0:T(8,128)(2,1)} %bitcast.138, pred[64,5]{1,0:T(8,128)(4,1)S(1)} %copy.41, f32[64,128]{1,0:T(8,128)S(1)} %bitcast.151), kind=kOutput, calls=%fused_computation.50 | convolution fusion | flops 337379328 | bytes 13664576 | tf_op jit(solution)/shard_map/rsij,vrsj->vri/dot_general | solution.py:27
  24.4 1.3 collective-permute-start.3
  25.7 8.2 %collective-permute-start.2 = (bf16[32,8192]{1,0:T(8,128)(2,1)S(1)}, bf16[32,8192]{1,0:T(8,128)(2,1)S(1)}, u32[]{:S(2)}, u32[]{:S(2)}) collective-permute-start(bf16[32,8192]{1,0:T(8,128)(2,1)S(1)} %bitcast.142), channel_id=1, source_target_pairs={{0,1},{1,2},{2,3},{3,4},{4,5},{5,6},{6,7},{7,8},{8,9},{9,10},{10,1... | collective-permute-start | bytes 1572872 | tf_op jit(solution)/shard_map/ppermute | solution.py:14
  34.0 1.5 %collective-permute-done.2 = bf16[32,8192]{1,0:T(8,128)(2,1)S(1)} collective-permute-done((bf16[32,8192]{1,0:T(8,128)(2,1)S(1)}, bf16[32,8192]{1,0:T(8,128)(2,1)S(1)}, u32[]{:S(2)}, u32[]{:S(2)}) %collective-permute-start.2) | collective-permute-done | bytes 524320 | tf_op jit(solution)/shard_map/ppermute | solution.py:14
  35.4 0.3 copy_bitcast_fusion.2
  35.7 3.0 %gather_fusion.1 = bf16[320,32,128]{2,1,0:T(8,128)(2,1)} fusion(bf16[32,192,128]{2,0,1:T(8,128)(2,1)S(1)} %copy_bitcast_fusion.2, s32[1024]{0:T(1024)S(1)} %pad_clamp_fusion), kind=kCustom, calls=%fused_computation.1.clone | custom fusion | bytes 5244160 | tf_op jit(solution)/shard_map/jit(_take)/gather | solution.py:26
  38.7 8.5 %fusion.47 = bf16[64,4,8,128]{3,2,1,0:T(8,128)(2,1)S(1)} fusion(bf16[64,5,128,128]{3,2,1,0:T(8,128)(2,1)} %param.6, bf16[64,5,32,128]{3,2,1,0:T(8,128)(2,1)} %bitcast.139, pred[64,5]{1,0:T(8,128)(4,1)S(1)} %copy.41, f32[64,128]{1,0:T(8,128)S(1)} %bitcast.152), kind=kOutput, calls=%fused_computation.49 | convolution fusion | flops 337379328 | bytes 13664576 | tf_op jit(solution)/shard_map/rsij,vrsj->vri/dot_general | solution.py:27
  47.3 1.3 collective-permute-start.5
  48.6 13.6 %collective-permute-start.4 = (bf16[32,8192]{1,0:T(8,128)(2,1)S(1)}, bf16[32,8192]{1,0:T(8,128)(2,1)S(1)}, u32[]{:S(2)}, u32[]{:S(2)}) collective-permute-start(bf16[32,8192]{1,0:T(8,128)(2,1)S(1)} %bitcast.145), channel_id=1, source_target_pairs={{0,1},{1,2},{2,3},{3,4},{4,5},{5,6},{6,7},{7,8},{8,9},{9,10},{10,1... | collective-permute-start | bytes 1572872 | tf_op jit(solution)/shard_map/ppermute | solution.py:14
  62.2 1.3 collective-permute-done.4
  63.5 0.3 copy_bitcast_fusion.1
  63.8 3.0 %gather_fusion.2 = bf16[320,32,128]{2,1,0:T(8,128)(2,1)} fusion(bf16[32,192,128]{2,0,1:T(8,128)(2,1)S(1)} %copy_bitcast_fusion.1, s32[1024]{0:T(1024)S(1)} %pad_clamp_fusion), kind=kCustom, calls=%fused_computation.2.clone | custom fusion | bytes 5244160 | tf_op jit(solution)/shard_map/jit(_take)/gather | solution.py:26
  66.8 8.5 %fusion.42 = bf16[64,4,8,128]{3,2,1,0:T(8,128)(2,1)S(1)} fusion(bf16[64,5,128,128]{3,2,1,0:T(8,128)(2,1)} %param.6, bf16[64,5,32,128]{3,2,1,0:T(8,128)(2,1)} %bitcast.140, pred[64,5]{1,0:T(8,128)(4,1)S(1)} %copy.41, f32[64,128]{1,0:T(8,128)S(1)} %bitcast.153), kind=kOutput, calls=%fused_computation.48 | convolution fusion | flops 337379328 | bytes 13664576 | tf_op jit(solution)/shard_map/rsij,vrsj->vri/dot_general | solution.py:27
  75.4 1.3 collective-permute-start.7
  76.7 10.6 %collective-permute-start.6 = (bf16[32,8192]{1,0:T(8,128)(2,1)S(1)}, bf16[32,8192]{1,0:T(8,128)(2,1)S(1)}, u32[]{:S(2)}, u32[]{:S(2)}) collective-permute-start(bf16[32,8192]{1,0:T(8,128)(2,1)S(1)} %bitcast.148), channel_id=1, source_target_pairs={{0,1},{1,2},{2,3},{3,4},{4,5},{5,6},{6,7},{7,8},{8,9},{9,10},{10,1... | collective-permute-start | bytes 1572872 | tf_op jit(solution)/shard_map/ppermute | solution.py:14
  87.3 1.5 %collective-permute-done.6 = bf16[32,8192]{1,0:T(8,128)(2,1)S(1)} collective-permute-done((bf16[32,8192]{1,0:T(8,128)(2,1)S(1)}, bf16[32,8192]{1,0:T(8,128)(2,1)S(1)}, u32[]{:S(2)}, u32[]{:S(2)}) %collective-permute-start.6) | collective-permute-done | bytes 524320 | tf_op jit(solution)/shard_map/ppermute | solution.py:14
  89.1 3.0 %gather_fusion.3 = bf16[320,32,128]{2,1,0:T(8,128)(2,1)} fusion(bf16[32,192,128]{2,0,1:T(8,128)(2,1)S(1)} %copy_bitcast_fusion, s32[1024]{0:T(1024)S(1)} %pad_clamp_fusion), kind=kCustom, calls=%fused_computation.3.clone | custom fusion | bytes 5244160 | tf_op jit(solution)/shard_map/jit(_take)/gather | solution.py:26
  92.1 8.4 %fusion.37 = f32[64,32,128]{2,1,0:T(8,128)S(1)} fusion(bf16[64,5,128,128]{3,2,1,0:T(8,128)(2,1)} %param.6, bf16[64,5,32,128]{3,2,1,0:T(8,128)(2,1)} %bitcast.137, pred[64,5]{1,0:T(8,128)(4,1)S(1)} %copy.41, f32[64,128]{1,0:T(8,128)S(1)} %bitcast.154), kind=kOutput, calls=%fused_computation.47 | convolution fusion | flops 337117184 | bytes 14188864 | tf_op jit(solution)/shard_map/rsij,vrsj->vri/dot_general | solution.py:27
  100.6 1.0 fusion.32
  101.5 35.3 %all-gather = f32[512,32]{1,0:T(8,128)S(1)} all-gather(f32[32,32]{1,0:T(8,128)S(1)} %fusion.32), channel_id=2, replica_groups=mesh['groups'=2,'rows'=16] {'rows'}, dimensions={0}, use_global_device_ids=true | all-gather | bytes 69632 | tf_op jit(solution)/shard_map/all_gather | solution.py:57
  137.0 2.9 %cholesky.16 = f32[32,32]{1,0:T(8,128)S(1)} custom-call(f32[32,32]{1,0:T(8,128)S(1)} %fusion.57), custom_call_target="Cholesky" | custom-call | tf_op jit(solution)/shard_map/jit(cholesky)/cholesky | solution.py:58
  139.9 0.6 compare_reduce_fusion
  140.6 0.7 fusion.55
  141.2 2.4 %custom-call.7 = f32[1,32,32]{1,2,0:T(8,128)S(1)} custom-call(f32[1,32,32]{2,1,0:T(8,128)S(1)} %fusion.55), custom_call_target="InvertDiagBlocksLowerTriangular" | custom-call | tf_op jit(solution)/shard_map/jit(_solve_triangular)/triangular_solve | solution.py:59
  143.6 1.1 fusion.33
  144.7 2.0 %convolution_bitcast_fusion = f32[32,8192]{1,0:T(8,128)} fusion(f32[32,8192]{1,0:T(8,128)S(1)} %fusion.33, f32[32,32]{1,0:T(8,128)S(1)} %copy-done), kind=kOutput, calls=%fused_computation.5 | convolution fusion | flops 100663296 | bytes 2101248 | tf_op jit(solution)/shard_map/dot_general | solution.py:60
  (24 shorter events, 1.1 us)
Async XLA Ops:
  0.0 144.7 %copy-start = (f32[32,32]{1,0:T(8,128)S(1)}, f32[32,32]{1,0:T(8,128)}, u32[]{:S(2)}) copy-start(f32[32,32]{1,0:T(8,128)} %param.9) | copy-start | bytes 12292
  0.0 11.5 %collective-permute-start = (bf16[32,8192]{1,0:T(8,128)(2,1)}, bf16[32,8192]{1,0:T(8,128)(2,1)S(1)}, u32[]{:S(2)}, u32[]{:S(2)}) collective-permute-start(bf16[32,8192]{1,0:T(8,128)(2,1)} %param.8), channel_id=1, source_target_pairs={{0,1},{1,2},{2,3},{3,4},{4,5},{5,6},{6,7},{7,8},{8,9},{9,10},{10,1... | collective-permute-start | bytes 1572872 | tf_op jit(solution)/shard_map/ppermute | solution.py:14
  2.5 8.9 %collective-permute-start.1 = (bf16[32,8192]{1,0:T(8,128)(2,1)}, bf16[32,8192]{1,0:T(8,128)(2,1)}, u32[]{:S(2)}, u32[]{:S(2)}) collective-permute-start(bf16[32,8192]{1,0:T(8,128)(2,1)} %param.8), channel_id=1, source_target_pairs={{1,0},{2,1},{3,2},{4,3},{5,4},{6,5},{7,6},{8,7},{9,8},{10,9},{11,1... | collective-permute-start | bytes 1572872 | tf_op jit(solution)/shard_map/ppermute | solution.py:17
  3.8 6.6 %copy-start.2 = (s32[64,5]{0,1:T(8,128)S(1)}, s32[64,5]{0,1:T(8,128)}, u32[]{:S(2)}) copy-start(s32[64,5]{0,1:T(8,128)} %param.7) | copy-start | bytes 3844
  3.8 7.6 %copy-start.1 = (bf16[32,8192]{1,0:T(8,128)(2,1)S(1)}, bf16[32,8192]{1,0:T(8,128)(2,1)}, u32[]{:S(2)}) copy-start(bf16[32,8192]{1,0:T(8,128)(2,1)} %param.8) | copy-start | bytes 1572868
  24.4 9.5 %collective-permute-start.3 = (bf16[32,8192]{1,0:T(8,128)(2,1)S(1)}, bf16[32,8192]{1,0:T(8,128)(2,1)S(1)}, u32[]{:S(2)}, u32[]{:S(2)}) collective-permute-start(bf16[32,8192]{1,0:T(8,128)(2,1)S(1)} %bitcast.141), channel_id=1, source_target_pairs={{1,0},{2,1},{3,2},{4,3},{5,4},{6,5},{7,6},{8,7},{9,8},{10,9},{11,1... | collective-permute-start | bytes 1572872 | tf_op jit(solution)/shard_map/ppermute | solution.py:17
  25.7 9.7 %collective-permute-start.2 = (bf16[32,8192]{1,0:T(8,128)(2,1)S(1)}, bf16[32,8192]{1,0:T(8,128)(2,1)S(1)}, u32[]{:S(2)}, u32[]{:S(2)}) collective-permute-start(bf16[32,8192]{1,0:T(8,128)(2,1)S(1)} %bitcast.142), channel_id=1, source_target_pairs={{0,1},{1,2},{2,3},{3,4},{4,5},{5,6},{6,7},{7,8},{8,9},{9,10},{10,1... | collective-permute-start | bytes 1572872 | tf_op jit(solution)/shard_map/ppermute | solution.py:14
  47.3 14.9 %collective-permute-start.5 = (bf16[32,8192]{1,0:T(8,128)(2,1)S(1)}, bf16[32,8192]{1,0:T(8,128)(2,1)S(1)}, u32[]{:S(2)}, u32[]{:S(2)}) collective-permute-start(bf16[32,8192]{1,0:T(8,128)(2,1)S(1)} %bitcast.144), channel_id=1, source_target_pairs={{1,0},{2,1},{3,2},{4,3},{5,4},{6,5},{7,6},{8,7},{9,8},{10,9},{11,1... | collective-permute-start | bytes 1572872 | tf_op jit(solution)/shard_map/ppermute | solution.py:17
  48.6 14.9 %collective-permute-start.4 = (bf16[32,8192]{1,0:T(8,128)(2,1)S(1)}, bf16[32,8192]{1,0:T(8,128)(2,1)S(1)}, u32[]{:S(2)}, u32[]{:S(2)}) collective-permute-start(bf16[32,8192]{1,0:T(8,128)(2,1)S(1)} %bitcast.145), channel_id=1, source_target_pairs={{0,1},{1,2},{2,3},{3,4},{4,5},{5,6},{6,7},{7,8},{8,9},{9,10},{10,1... | collective-permute-start | bytes 1572872 | tf_op jit(solution)/shard_map/ppermute | solution.py:14
  75.4 11.9 %collective-permute-start.7 = (bf16[32,8192]{1,0:T(8,128)(2,1)S(1)}, bf16[32,8192]{1,0:T(8,128)(2,1)S(1)}, u32[]{:S(2)}, u32[]{:S(2)}) collective-permute-start(bf16[32,8192]{1,0:T(8,128)(2,1)S(1)} %bitcast.147), channel_id=1, source_target_pairs={{1,0},{2,1},{3,2},{4,3},{5,4},{6,5},{7,6},{8,7},{9,8},{10,9},{11,1... | collective-permute-start | bytes 1572872 | tf_op jit(solution)/shard_map/ppermute | solution.py:17
  76.7 12.1 %collective-permute-start.6 = (bf16[32,8192]{1,0:T(8,128)(2,1)S(1)}, bf16[32,8192]{1,0:T(8,128)(2,1)S(1)}, u32[]{:S(2)}, u32[]{:S(2)}) collective-permute-start(bf16[32,8192]{1,0:T(8,128)(2,1)S(1)} %bitcast.148), channel_id=1, source_target_pairs={{0,1},{1,2},{2,3},{3,4},{4,5},{5,6},{6,7},{7,8},{8,9},{9,10},{10,1... | collective-permute-start | bytes 1572872 | tf_op jit(solution)/shard_map/ppermute | solution.py:14
